TPU v7x, 512 devices: a whole 4x8x8 slice. The times are simulated.
512 devices in a mesh: group: 8 (over x, core), member: 64 (over y, z).
Axes of the slice: x: 4, y: 8, z: 8, core: 2. Of those that a mesh axis runs over, the one named last changes fastest.
Arguments:
- queries: bfloat16 [24576, 4096], P(('group', 'member')), may hold values from -48 to 48
- passages: bfloat16 [2048, 4096], P(('group', 'member')), may hold values from -6 to 6
- pool: bfloat16 [65536, 4096], P(('group', 'member')), may hold values from -6 to 6
- positives: int32 [24576], P(('group', 'member')), may hold values from 0 to 255
- weights: float32 [24576], P(('group', 'member')), may hold values from 4 to 64
- requests: int32 [512, 8], P(('group', 'member')), may hold values from 0 to 1, as said below
Outputs:
- grad_queries: bfloat16 [24576, 4096], P(('group', 'member'))
- grad_passages: bfloat16 [2048, 4096], P(('group', 'member'))
- grad_pool: bfloat16 [65536, 4096], P(('group', 'member'))
Inputs may be any that keep to these rules, and one draw needn't show every extreme that they name: `requests`: 0 in the column of the block's own group.
All inputs are finite; a program needn't handle non-finite values.
Results may differ from a plain program's by a relative error of at most 0.0065.
Values may be sent and summed in bfloat16 or wider, within the bound.
A program may use at most 64 MiB of HBM per device.

v0:
```python
import jax
import jax.numpy as jnp
from jax import lax
from jax.sharding import PartitionSpec as P


def visit_scores(visitors, asked, pool, own_group, factor, query_count):
    group_count = asked.shape[0]
    picker = (jnp.arange(group_count, dtype=jnp.int32)[None, :] == own_group).astype(jnp.int32)
    column = jnp.sum(asked * picker, axis=1)
    row_mask = jnp.repeat(column != 0, query_count)
    scores = jnp.einsum("qd,hd->qh", visitors, pool, preferred_element_type=jnp.float32) * factor
    return (jnp.where(row_mask[:, None], scores, -1e30), row_mask)


def visit_coefs(scores, visit_weights, visit_logsum, factor):
    return (visit_weights[:, None] * jnp.exp(scores - visit_logsum[:, None]) * factor).astype(
        jnp.bfloat16
    )


def per_device(queries, passages, pool, positives, weights, requests):
    own_group = lax.axis_index("group")
    query_count, width = queries.shape
    block_rows = pool.shape[0]
    factor = width ** (-0.5)
    batch = lax.all_gather(passages, "member", axis=0, tiled=True)
    in_scores = jnp.einsum("qd,pd->qp", queries, batch, preferred_element_type=jnp.float32) * factor
    one_hot = (jnp.arange(batch.shape[0], dtype=jnp.int32)[None, :] == positives[:, None]).astype(
        jnp.float32
    )
    blocks = lax.all_gather(pool, "group", axis=0, tiled=True)
    wanted = jnp.repeat(requests[0] != 0, block_rows)
    hard_scores = (
        jnp.einsum("qd,hd->qh", queries, blocks, preferred_element_type=jnp.float32) * factor
    )
    hard_scores = jnp.where(wanted[None, :], hard_scores, -1e30)
    highest = jnp.maximum(jnp.max(in_scores, axis=1), jnp.max(hard_scores, axis=1))
    totals = jnp.sum(jnp.exp(in_scores - highest[:, None]), axis=1)
    totals = totals + jnp.sum(jnp.exp(hard_scores - highest[:, None]), axis=1)
    logsum = highest + jnp.log(totals)
    in_coefs = (
        weights[:, None] * (jnp.exp(in_scores - logsum[:, None]) - one_hot) * factor
    ).astype(jnp.bfloat16)
    near_coefs = (weights[:, None] * jnp.exp(hard_scores - logsum[:, None]) * factor).astype(
        jnp.bfloat16
    )
    grad_rows = jnp.dot(in_coefs, batch, preferred_element_type=jnp.float32)
    grad_rows = grad_rows + jnp.dot(near_coefs, blocks, preferred_element_type=jnp.float32)
    visitors, asked = (
        lax.all_gather(queries, "group", axis=0, tiled=True),
        lax.all_gather(requests, "group", axis=0, tiled=True),
    )
    visit_weights, visit_logsum = (
        lax.all_gather(weights, "group", axis=0, tiled=True),
        lax.all_gather(logsum, "group", axis=0, tiled=True),
    )
    scores, row_mask = visit_scores(visitors, asked, pool, own_group, factor, query_count)
    far_coefs = visit_coefs(scores, visit_weights, visit_logsum, factor)
    grad_pool = jnp.einsum("qh,qd->hd", far_coefs, visitors, preferred_element_type=jnp.float32)
    grad_passages = lax.psum_scatter(
        jnp.einsum("qp,qd->pd", in_coefs, queries, preferred_element_type=jnp.float32),
        "member",
        scatter_dimension=0,
        tiled=True,
    )
    return (
        grad_rows.astype(jnp.bfloat16),
        grad_passages.astype(jnp.bfloat16),
        grad_pool.astype(jnp.bfloat16),
    )


def solution(mesh):
    placed = (
        P(("group", "member"), None),
        P(("group", "member"), None),
        P(("group", "member"), None),
        P(("group", "member")),
        P(("group", "member")),
        P(("group", "member"), None),
    )
    return jax.shard_map(
        per_device,
        mesh=mesh,
        in_specs=placed,
        out_specs=(
            P(("group", "member"), None),
            P(("group", "member"), None),
            P(("group", "member"), None),
        ),
        check_vma=False,
    )
```

profile of v0, /device:TPU:2, one launch (start us, length us, event | category | flops | bytes accessed | tf_op | source)
XLA Modules:
  0.0 525.1 jit_solution(13657396400033851462)
XLA Ops:
  7.2 0.7 all-gather.10.cloned.1.call-update
  8.0 0.7 all-gather.6.cloned.1.call-update
  8.7 0.7 all-gather.8.cloned.1.call-update
  9.4 13.8 %all-gather.1 = s32[8,1,8]{2,1,0:T(1,128)S(1)} all-gather(s32[1,1,8]{2,1,0:T(1,128)} %bitcast.21), channel_id=1, replica_groups=mesh['group'=8,'member'=64] {'group'}, dimensions={0}, use_global_device_ids=true | all-gather | bytes 288 | tf_op jit(solution)/shard_map/all_gather | solution.py:52
  23.2 0.1 multiply_reduce_fusion
  23.5 1.3 dynamic-slice
  25.4 1.3 dynamic-slice.2
  27.3 0.9 dynamic-update-slice
  28.2 0.7 compare_bitcast_fusion
  28.9 70.5 %all-gather.10.cloned.1.call-done = bf16[64,4,4096]{2,1,0:T(4,128)(2,1)} async-done(((bf16[1,4,4096]{2,1,0:T(4,128)(2,1)}), bf16[64,4,4096]{2,1,0:T(4,128)(2,1)}) %all-gather.10.cloned.1.call-update) | async-done | bytes 2097168 | tf_op jit(solution)/shard_map/all_gather | solution.py:27
  99.4 2.5 reshape.44
  102.0 0.8 fusion.22
  102.9 49.8 %all-gather.6.cloned.1.call-done = bf16[1024,4096]{1,0:T(8,128)(2,1)} async-done(((bf16[128,4096]{1,0:T(8,128)(2,1)}), bf16[1024,4096]{1,0:T(8,128)(2,1)}) %all-gather.6.cloned.1.call-update) | async-done | bytes 8388624 | tf_op jit(solution)/shard_map/all_gather | solution.py:32
  152.7 6.1 %fusion.23 = (f32[48]{0:T(128)S(1)}, f32[48,1024]{1,0:T(8,128)S(1)}) fusion(bf16[48,4096]{1,0:T(8,128)(2,1)S(1)} %copy-done, bf16[1024,4096]{1,0:T(8,128)(2,1)} %all-gather.6.cloned.1.call-done, pred[1024]{0:T(1024)(128)(4,1)S(1)} %broadcast_bitcast_fusion), kind=kOutput, calls=%fused_computation.40 | convolution fusion | flops 402800576 | bytes 8979648 | tf_op jit(solution)/shard_map/qd,hd->qh/dot_general | solution.py:35
  158.8 0.2 exponential_reduce_fusion.1
  159.0 0.2 exponential_reduce_fusion
  159.2 0.1 fusion.21
  159.3 2.8 fusion.19
  162.1 11.2 %all-reduce.3 = (f32[384]{0:T(512)S(1)}, f32[384]{0:T(512)S(1)}) all-reduce(f32[384]{0:T(512)S(1)} %get-tuple-element.5, f32[384]{0:T(512)S(1)} %dynamic-update-slice), channel_id=1, replica_groups=mesh['group'=8,'member'=64] {'group'}, use_global_device_ids=true, to_apply=%add.1 | all-reduce | flops 768 | bytes 6144
  173.3 0.5 fusion.20
  173.8 331.8 %all-reduce.5 = bf16[256,4096]{1,0:T(8,128)(2,1)S(1)} all-reduce(f32[256,4096]{1,0:T(8,128)} %fusion.19), channel_id=2, replica_groups=mesh['group'=8,'member'=64] {'member'}, use_global_device_ids=true, to_apply=%region_4.5.clone | all-reduce | flops 1048576 | bytes 6291456
  505.6 0.6 dynamic-slice_convert_fusion
  506.2 5.8 %fusion = bf16[48,4096]{1,0:T(8,128)(2,1)} fusion(f32[48,4096]{1,0:T(8,128)S(1)} %fusion.20, bf16[1024,4096]{1,0:T(8,128)(2,1)} %all-gather.6.cloned.1.call-done, f32[48,1024]{1,0:T(8,128)S(1)} %get-tuple-element.10, f32[48]{0:T(128)S(1)} %get-tuple-element.6, f32[48]{0:T(128)S(1)} %copy-done.2), kind=kOutput, calls=%fused_computation.2 | convolution fusion | flops 403243008 | bytes 9765248 | tf_op jit(solution)/shard_map/dot_general | solution.py:49
  512.1 6.6 %convolution_convert_fusion = bf16[128,4096]{1,0:T(8,128)(2,1)} fusion(bf16[384,4096]{1,0:T(8,128)(2,1)} %all-gather.8.cloned.1.call-done, bf16[128,4096]{1,0:T(8,128)(2,1)S(1)} %copy-done.1, f32[384]{0:T(512)S(1)} %get-tuple-element.3, f32[384]{0:T(512)S(1)} %get-tuple-element.4, pred[384]{0:T(512)(128)(4,1)S(1)} %broadcast_in_dim.50), kind=kOutput, calls=%fused_computation | convolution fusion | flops 806125568 | bytes 5246336 | tf_op jit(solution)/shard_map/qh,qd->hd/dot_general | solution.py:60
  (20 shorter events, 0.4 us)
Async XLA Ops:
  7.2 94.8 %copy-start = (bf16[48,4096]{1,0:T(8,128)(2,1)S(1)}, bf16[48,4096]{1,0:T(8,128)(2,1)}, u32[]{:S(2)}) copy-start(bf16[48,4096]{1,0:T(8,128)(2,1)} %param.6) | copy-start | bytes 1179652
  7.2 92.3 %all-gather.10.cloned.1.call-start = ((), (), s32[]{:S(2)}) async-start(), calls=%async_computation.2 | async-start | bytes 2129920 | tf_op jit(solution)/shard_map/all_gather | solution.py:27
  7.9 144.7 %all-gather.6.cloned.1.call-start = ((), (), s32[]{:S(2)}) async-start(), calls=%async_computation | async-start | bytes 9437184 | tf_op jit(solution)/shard_map/all_gather | solution.py:32
  8.7 503.4 %all-gather.8.cloned.1.call-start = ((), (), s32[]{:S(2)}) async-start(), calls=%async_computation.1 | async-start | bytes 3538944 | tf_op jit(solution)/shard_map/all_gather | solution.py:51
  102.9 56.5 %copy-start.2 = (f32[48]{0:T(128)S(1)}, f32[48]{0:T(128)}, u32[]{:S(2)}) copy-start(f32[48]{0:T(128)} %param.10) | copy-start | bytes 580
  102.9 56.4 %copy-start.3 = (s32[48]{0:T(128)S(1)}, s32[48]{0:T(128)}, u32[]{:S(2)}) copy-start(s32[48]{0:T(128)} %param.9) | copy-start | bytes 580
  506.2 5.8 %copy-start.1 = (bf16[128,4096]{1,0:T(8,128)(2,1)S(1)}, bf16[128,4096]{1,0:T(8,128)(2,1)}, u32[]{:S(2)}) copy-start(bf16[128,4096]{1,0:T(8,128)(2,1)} %param.8) | copy-start | bytes 3145732
Sparse Core Ops, SparseCore 0:
  11.0 88.3 all-gather.9
  101.6 51.0 all-gather.5
  154.8 33.0 all-gather.7
where the time goes:
time: 526 us; the launch traced here: 525 us
  blocking collectives  357 us (68%)
  waiting for transfers between devices  122 us (23%)
  matrix products  22.7 us (4%)
  between operations  15.2 us (3%)
  local copies, waits for them, and re-layouts  6.84 us (1%)
    unnamed x2, blocking collectives  343 us
    all_gather x1, waiting for transfers between devices, per_device(): batch = lax.all_gather(passages, 'member', axis=0, tiled=True)  70.5 us
    all_gather x1, waiting for transfers between devices, per_device(): blocks = lax.all_gather(pool, 'group', axis=0, tiled=True)  49.8 us
    all_gather x1, blocking collectives, per_device(): lax.all_gather(requests, 'group', axis=0, tiled=True)  13.8 us
  transfers between devices with their start and end apart: 3, of which 2 were waited for; matrix products, arithmetic and copies ran while one was open for 5% of the time, Pallas kernels for 0%

commit v1 on v0

v1 whole, which is shorter than its diff:
```python
import functools

import jax
import jax.numpy as jnp
from jax import lax
from jax.experimental import pallas as pl
from jax.experimental.pallas import tpu as pltpu
from jax.sharding import PartitionSpec as P

MESH = pl.DeviceIdType.MESH
F32 = jnp.float32
BF16 = jnp.bfloat16

D = 4096
Q = 48
HB = 128
W = 1024
HW = 512
QW = 256
HALF = D // 2
N = 8
HOPS = N // 2
FACTOR = D ** (-0.5)
NEG = -1e30


def nt(a, b):
    return lax.dot_general(a, b, (((1,), (1,)), ((), ())), preferred_element_type=F32)


def nn(a, b):
    return lax.dot_general(a, b, (((1,), (0,)), ((), ())), preferred_element_type=F32)


def tn(a, b):
    return lax.dot_general(a, b, (((0,), (0,)), ((), ())), preferred_element_type=F32)


def loop(n, body):
    lax.fori_loop(0, n, lambda i, _: (body(i), 0)[1], 0)


def cols(i, size):
    return pl.ds(pl.multiple_of(i * size, size), size)


def kernel(
    q_ref, p_ref, pool_ref, pos_ref, w_ref, req_ref,
    gq_ref, gp_ref, gpool_ref,
    q_all, pool2, ga, gb, meta, sc, pb, part, fw, rx, st_out, st, sto, ls,
    q4, tin, cin, gpa, gpb, ra, rb, rah, rbh, sa, sb, sa_in, sb_in,
    gq_acc, gq_out, cb, gpo_out, gpo_in, gpo_acc, gpo_done, gp_done,
    loc, qs, qr, ps, pr, ms, mr, a1s, a1r, b1s, b1r, ags, agr, sts, str_, lss, lsr,
    pts, ptr, gps, gpr, rss, rsr, a2s, a2r, b2s, b2r,
):
    g = lax.axis_index("group")
    mem = lax.axis_index("member")
    x, c = lax.div(g, 2), lax.rem(g, 2)
    y, z = lax.div(mem, N), lax.rem(mem, N)
    right = (lax.rem(x + 1, 4) * 2 + c, mem)
    left = (lax.rem(x + 3, 4) * 2 + c, mem)
    opp = (lax.rem(x + 2, 4) * 2 + c, mem)
    mate_group = x * 2 + 1 - c
    mate = (mate_group, mem)

    def yd(d):
        return (g, lax.rem(y + d, N) * N + z)

    def zd(d):
        return (g, y * N + lax.rem(z + d, N))

    def rc(src, dst, ssem, rsem, dev):
        return pltpu.make_async_remote_copy(
            src_ref=src, dst_ref=dst, send_sem=ssem, recv_sem=rsem,
            device_id=dev, device_id_type=MESH,
        )

    sent = []

    def go(copy):
        copy.start()
        sent.append(copy)

    barrier = pltpu.get_barrier_semaphore()
    for dev in (right, left, opp, mate):
        pl.semaphore_signal(barrier, inc=1, device_id=dev, device_id_type=MESH)
    for d in range(1, N):
        pl.semaphore_signal(barrier, inc=1, device_id=yd(d), device_id_type=MESH)
        pl.semaphore_signal(barrier, inc=1, device_id=zd(d), device_id_type=MESH)

    load_q = pltpu.make_async_copy(q_ref, q_all.at[0], loc.at[0])
    load_pool = pltpu.make_async_copy(pool_ref, pool2.at[pl.ds(0, HB)], loc.at[1])
    load_q.start()
    load_pool.start()

    pf = p_ref[...].astype(F32)
    row16 = lax.broadcasted_iota(jnp.int32, (16, HW), 0)

    def fold(off):
        acc = jnp.zeros((16, HW), F32)
        for r in range(4):
            for k in range(4):
                piece = pf[r:r + 1, k * W + off:k * W + off + HW]
                acc = jnp.where(row16 == 4 * r + k, piece, acc)
        return acc.astype(BF16)

    ga[y, z] = fold(0)
    gb[y, z] = fold(HW)
    meta[0] = jnp.zeros((8, 128), F32)
    meta[0, 0:1, 0:8] = req_ref[...].astype(F32)

    pl.semaphore_wait(barrier, 4 + 2 * (N - 1))

    for d in range(1, N):
        go(rc(ga.at[y, z], ga.at[y, z], a1s.at[d], a1r.at[d], zd(d)))
        go(rc(gb.at[y, z], gb.at[y, z], b1s.at[d], b1r.at[d], yd(d)))
    h0, h1 = pl.ds(0, HALF), pl.ds(HALF, HALF)
    go(rc(q_ref.at[:, h0], q_all.at[1, :, h0], qs.at[0], qr.at[0], right))
    go(rc(q_ref.at[:, h1], q_all.at[2, :, h1], qs.at[2], qr.at[2], left))
    go(rc(meta.at[0], meta.at[1], ms.at[0], mr.at[0], right))
    go(rc(meta.at[0], meta.at[2], ms.at[1], mr.at[1], left))
    go(rc(meta.at[0], meta.at[3], ms.at[2], mr.at[2], opp))
    go(rc(pool_ref, pool2.at[pl.ds(HB, HB)], ps.at[0], pr.at[0], mate))
    go(rc(q_ref.at[:, h1], q_all.at[1, :, h1], qs.at[1], qr.at[1], right))
    go(rc(q_ref.at[:, h0], q_all.at[2, :, h0], qs.at[3], qr.at[3], left))

    def arrived(ref, sem):
        rc(ref, ref, sem, sem, right).wait_recv()

    def ring(flow, d):
        sign = 1 if flow % 2 == 0 else -1
        if flow < 2:
            blk = lax.rem(y - sign * d + N, N)
            if d == HOPS:
                return ga.at[blk, :, :, pl.ds(0 if sign > 0 else QW, QW)]
            return ga.at[blk]
        blk = lax.rem(z - sign * d + N, N)
        if d == HOPS:
            return gb.at[:, blk, :, pl.ds(0 if sign > 0 else QW, QW)]
        return gb.at[:, blk]

    def ring_send(d):
        for flow in range(4):
            sign = 1 if flow % 2 == 0 else -1
            if flow < 2:
                blk = lax.rem(y - sign * (d - 1) + N, N)
                src = ga.at[blk]
                if d == HOPS:
                    src = ga.at[blk, :, :, pl.ds(0 if sign > 0 else QW, QW)]
                dev = yd(1 if sign > 0 else N - 1)
            else:
                blk = lax.rem(z - sign * (d - 1) + N, N)
                src = gb.at[:, blk]
                if d == HOPS:
                    src = gb.at[:, blk, :, pl.ds(0 if sign > 0 else QW, QW)]
                dev = zd(1 if sign > 0 else N - 1)
            if d > 1:
                arrived(ring(flow, d - 1), agr.at[flow, d - 2])
            go(rc(src, src, ags.at[flow, d - 1], agr.at[flow, d - 1], dev))

    for d in range(1, N):
        src = lax.rem(z + N - d, N)
        arrived(ga.at[y, src], a1r.at[d])
        src = lax.rem(y + N - d, N)
        arrived(gb.at[src, z], b1r.at[d])
    ring_send(1)

    lane256 = lax.broadcasted_iota(jnp.int32, (1, 2 * HB), 1)
    lane128 = lax.broadcasted_iota(jnp.int32, (1, 128), 1)

    def hard(slot):
        def body(i, acc):
            at = cols(i, 1024)
            return acc + nt(q_all[slot, :, at], pool2[:, at])

        scores = lax.fori_loop(0, 4, body, jnp.zeros((Q, 2 * HB), F32)) * FACTOR
        line = meta[slot, 0:1, :]
        here = jnp.sum(jnp.where(lane128 == g, line, 0.0), axis=1, keepdims=True)
        there = jnp.sum(jnp.where(lane128 == mate_group, line, 0.0), axis=1, keepdims=True)
        asked = jnp.where(lane256 < HB, here, there) != 0.0
        scores = jnp.where(asked, scores, NEG)
        sc[slot] = scores
        top = jnp.max(scores, axis=1, keepdims=True)
        probs = jnp.where(asked, jnp.exp(scores - top), 0.0)
        total = jnp.sum(probs, axis=1, keepdims=True)
        pb[slot] = probs.astype(BF16)
        st_out[slot] = jnp.where(lane128 < 64, top, total)

    arrived(q_all.at[1, :, h0], qr.at[0])
    go(rc(q_all.at[1, :, h0], q_all.at[3, :, h0], qs.at[4], qr.at[4], right))
    arrived(q_all.at[2, :, h1], qr.at[2])
    go(rc(q_all.at[2, :, h1], q_all.at[3, :, h1], qs.at[5], qr.at[5], left))

    load_q.wait()
    load_pool.wait()
    arrived(pool2.at[pl.ds(HB, HB)], pr.at[0])
    hard(0)
    for k in range(4):
        q4[0, k * Q:(k + 1) * Q, :] = q_all[0, :, k * W:k * W + HW]
        q4[1, k * Q:(k + 1) * Q, :] = q_all[0, :, k * W + HW:(k + 1) * W]
    ring_send(2)

    arrived(q_all.at[1, :, h1], qr.at[1])
    arrived(meta.at[1], mr.at[0])
    hard(1)
    go(rc(st_out.at[1], st.at[2], sts.at[0], str_.at[0], left))
    arrived(q_all.at[2, :, h0], qr.at[3])
    arrived(meta.at[2], mr.at[1])
    hard(2)
    go(rc(st_out.at[2], st.at[1], sts.at[1], str_.at[1], right))
    ring_send(3)

    arrived(q_all.at[3, :, h0], qr.at[4])
    arrived(q_all.at[3, :, h1], qr.at[5])
    arrived(meta.at[3], mr.at[2])
    hard(3)
    go(rc(st_out.at[3], st.at[3], sts.at[2], str_.at[2], opp))
    go(rc(st_out.at[3], sto.at[0], sts.at[3], str_.at[3], right))
    go(rc(st_out.at[3], sto.at[1], sts.at[4], str_.at[4], left))

    def partial(slot, first):
        def body(i):
            at = cols(i + first, 512)
            part[slot, :, at] = nn(pb[slot], pool2[:, at]).astype(BF16)

        loop(4, body)

    partial(3, 0)
    go(rc(part.at[3, :, h0], fw.at[0], pts.at[0], ptr.at[0], right))
    partial(3, 4)
    go(rc(part.at[3, :, h1], fw.at[1], pts.at[1], ptr.at[1], left))
    ring_send(4)
    partial(1, 0)
    go(rc(part.at[1, :, h0], rx.at[1, :, h0], pts.at[2], ptr.at[2], left))
    partial(2, 4)
    go(rc(part.at[2, :, h1], rx.at[0, :, h1], pts.at[3], ptr.at[3], right))

    for flow in range(4):
        arrived(ring(flow, HOPS), agr.at[flow, HOPS - 1])
    mod4 = lax.rem(lane256, 4)

    def in_block(b):
        pa = ga[pl.ds(2 * b, 2)].reshape(256, HW)
        pbk = gb[pl.ds(2 * b, 2)].reshape(256, HW)
        s = nt(q4[0], pa) + nt(q4[1], pbk)
        t = jnp.where(mod4 == 0, s[0:Q], 0.0)
        for k in range(1, 4):
            t = jnp.where(mod4 == k, s[k * Q:(k + 1) * Q], t)
        t = t + jnp.where(lax.rem(mod4, 2) == 0, pltpu.roll(t, 255, 1), pltpu.roll(t, 1, 1))
        t = t + jnp.where(mod4 < 2, pltpu.roll(t, 254, 1), pltpu.roll(t, 2, 1))
        tin[:, cols(b, 256)] = t * FACTOR

    loop(4, in_block)

    for i in range(3):
        arrived(st.at[(2, 1, 3)[i]], str_.at[i])
    tops = [st_out[0][:, 0:1]] + [st[i][:, 0:1] for i in (1, 2, 3)]
    sums = [st_out[0][:, 64:65]] + [st[i][:, 64:65] for i in (1, 2, 3)]
    t_in = tin[...]
    in_top = jnp.max(t_in, axis=1, keepdims=True)
    highest = in_top
    for t in tops:
        highest = jnp.maximum(highest, t)
    lane1024 = lax.broadcasted_iota(jnp.int32, (1, W), 1)
    in_sum = jnp.sum(
        jnp.where(lax.rem(lane1024, 4) == 0, jnp.exp(t_in - highest), 0.0), axis=1, keepdims=True
    )
    totals = in_sum
    for t, s in zip(tops, sums):
        totals = totals + s * jnp.exp(t - highest)
    logsum = highest + jnp.log(totals)
    eye = lax.broadcasted_iota(jnp.int32, (Q, Q), 0) == lax.broadcasted_iota(jnp.int32, (Q, Q), 1)
    weight = jnp.sum(jnp.where(eye, w_ref[...], 0.0), axis=1, keepdims=True)
    positive = jnp.sum(jnp.where(eye, pos_ref[...], 0), axis=1, keepdims=True)
    ls[0] = jnp.where(lane128 < 64, logsum, weight)
    go(rc(ls.at[0], ls.at[1], lss.at[0], lsr.at[0], right))
    go(rc(ls.at[0], ls.at[2], lss.at[1], lsr.at[1], left))
    go(rc(ls.at[0], ls.at[3], lss.at[2], lsr.at[2], opp))

    one_hot = (lax.div(lane1024, 4) == positive).astype(F32)
    coefs = weight * (jnp.exp(t_in - logsum) - one_hot) * FACTOR
    for k in range(4):
        cin[k * Q:(k + 1) * Q, :] = jnp.where(lax.rem(lane1024, 4) == k, coefs, 0.0).astype(BF16)

    def gp_block(b):
        cc = cin[:, cols(b, 128)]
        gpa[b] = tn(cc, q4[0]).astype(BF16).reshape(N, 16, HW)
        gpb[b] = tn(cc, q4[1]).astype(BF16).reshape(N, 16, HW)

    loop(N, gp_block)

    def chunk(flow, d):
        sign = 1 if flow % 2 == 0 else -1
        if flow < 2:
            return gpa, lax.rem(z + sign * d + N, N), 1
        return gpb, lax.rem(y + sign * d + N, N), 0

    def rs_view(flow, d, half):
        ref, blk, axis = chunk(flow, d)
        at = pl.ds(0 if flow % 2 == 0 else QW, QW) if half else pl.ds(0, HW)
        return ref.at[:, blk, :, at] if axis == 1 else ref.at[blk, :, :, at]

    def rs_slot(flow, s):
        if s == 0:
            return (rah if flow < 2 else rbh).at[flow % 2]
        return (ra if flow < 2 else rb).at[flow % 2, s - 1]

    def rs_dev(flow):
        d = 1 if flow % 2 == 0 else N - 1
        return zd(d) if flow < 2 else yd(d)

    def rs_send(s):
        for flow in range(4):
            if s > 0:
                arrived(rs_slot(flow, s - 1), rsr.at[flow, s - 1])
                dst = rs_view(flow, HOPS - s, s == 1)
                dst[...] = dst[...] + rs_slot(flow, s - 1)[...]
            go(rc(
                rs_view(flow, HOPS - s, s == 0), rs_slot(flow, s),
                rss.at[flow, s], rsr.at[flow, s], rs_dev(flow),
            ))

    rs_send(0)

    def merge(slot, way, first, dest, sem):
        arrived(sto.at[way], str_.at[3 + way])
        arrived(fw.at[way], ptr.at[way])
        mine, theirs = st_out[slot][:, 0:1], sto[way][:, 0:1]
        most = jnp.maximum(mine, theirs)
        a, b = jnp.exp(mine - most), jnp.exp(theirs - most)

        def body(i):
            at = cols(i + first, 512)
            own = nn(pb[slot], pool2[:, at])
            part[slot, :, at] = (own * a + fw[way, :, cols(i, 512)].astype(F32) * b).astype(BF16)

        loop(4, body)
        half = pl.ds(first * 512, HALF)
        go(rc(part.at[slot, :, half], rx.at[way, :, half], pts.at[sem], ptr.at[sem], dest))

    merge(2, 0, 0, right, 4)
    merge(1, 1, 4, left, 5)

    rs_send(1)

    for i in range(3):
        arrived(ls.at[i + 1], lsr.at[i])
    for slot in range(4):
        lsum, wt = ls[slot][:, 0:1], ls[slot][:, 64:65]
        cb[slot * Q:(slot + 1) * Q, :] = (wt * jnp.exp(sc[slot] - lsum) * FACTOR).astype(BF16)

    def far_pool(i):
        at = cols(i, 512)
        gpo_out[:, at] = tn(cb[:, HB:2 * HB], q_all[:, :, at].reshape(4 * Q, 512)).astype(BF16)

    loop(8, far_pool)
    go(rc(gpo_out, gpo_in, gps.at[0], gpr.at[0], mate))

    rs_send(2)

    def near_pool(i):
        at = cols(i, 512)
        gpo_acc[:, at] = tn(cb[:, 0:HB], q_all[:, :, at].reshape(4 * Q, 512))

    loop(8, near_pool)

    rs_send(3)

    def own_rows(i):
        at = cols(i, 512)
        gq_acc[:, at] = nn(cb[0:Q, :], pool2[:, at])

    loop(8, own_rows)

    for flow in range(4):
        arrived(rs_slot(flow, HOPS - 1), rsr.at[flow, HOPS - 1])
    sa[...] = (
        gpa[:, z].astype(F32) + ra[0, HOPS - 2].astype(F32) + ra[1, HOPS - 2].astype(F32)
    ).astype(BF16)
    sb[...] = (
        gpb[y].astype(F32) + rb[0, HOPS - 2].astype(F32) + rb[1, HOPS - 2].astype(F32)
    ).astype(BF16)
    for d in range(1, N):
        go(rc(sa.at[lax.rem(y + d, N)], sa_in.at[d], a2s.at[d], a2r.at[d], yd(d)))
        go(rc(sb.at[lax.rem(z + d, N)], sb_in.at[d], b2s.at[d], b2r.at[d], zd(d)))

    for h, ref in ((0, ga), (1, gb)):
        for n in range(2):
            at = pl.ds(n * QW, QW)
            rows = nn(cin[...], ref[:, :, :, at].reshape(W, QW))
            for k in range(4):
                to = pl.ds(k * W + h * HW + n * QW, QW)
                gq_acc[:, to] = gq_acc[:, to] + rows[k * Q:(k + 1) * Q]

    arrived(gpo_in, gpr.at[0])

    def pool_sum(i):
        at = cols(i, 512)
        gpo_done[:, at] = (gpo_acc[:, at] + gpo_in[:, at].astype(F32)).astype(BF16)

    loop(8, pool_sum)
    store_pool = pltpu.make_async_copy(gpo_done, gpool_ref, loc.at[2])
    store_pool.start()

    scale = weight * FACTOR

    def back(t):
        return scale * jnp.exp(t - logsum)

    t_l, t_r, t_o = tops[1], tops[2], tops[3]
    arrived(rx.at[1, :, h0], ptr.at[2])
    arrived(rx.at[0, :, h1], ptr.at[3])
    arrived(rx.at[0, :, h0], ptr.at[4])
    arrived(rx.at[1, :, h1], ptr.at[5])

    def finish(first, e_l, e_r):
        def body(i):
            at = cols(i + first, 512)
            gq_out[:, at] = (
                gq_acc[:, at] + rx[0, :, at].astype(F32) * e_l + rx[1, :, at].astype(F32) * e_r
            ).astype(BF16)

        loop(4, body)

    finish(0, back(jnp.maximum(t_l, t_o)), back(t_r))
    finish(4, back(t_l), back(jnp.maximum(t_r, t_o)))
    store_q = pltpu.make_async_copy(gq_out, gq_ref, loc.at[3])
    store_q.start()

    row4 = lax.broadcasted_iota(jnp.int32, (4, HW), 0)
    for h, own, held, sem in ((0, sa[y], sa_in, a2r), (1, sb[z], sb_in, b2r)):
        acc = own.astype(F32)
        for d in range(1, N):
            arrived(held.at[d], sem.at[d])
            acc = acc + held[d].astype(F32)
        for k in range(4):
            out = jnp.zeros((4, HW), F32)
            for r in range(4):
                out = jnp.where(row4 == r, acc[4 * r + k:4 * r + k + 1, :], out)
            gp_done[:, k * W + h * HW:k * W + (h + 1) * HW] = out.astype(BF16)
    store_p = pltpu.make_async_copy(gp_done, gp_ref, loc.at[4])
    store_p.start()

    for copy in sent:
        copy.wait_send()
    store_pool.wait()
    store_q.wait()
    store_p.wait()


def per_device(queries, passages, pool, positives, weights, requests):
    dma = pltpu.SemaphoreType.DMA
    v = pltpu.VMEM
    scratch = [
        v((4, Q, D), BF16),
        v((2 * HB, D), BF16),
        v((N, N, 16, HW), BF16),
        v((N, N, 16, HW), BF16),
        v((4, 8, 128), F32),
        v((4, Q, 2 * HB), F32),
        v((4, Q, 2 * HB), BF16),
        v((4, Q, D), BF16),
        v((2, Q, HALF), BF16),
        v((2, Q, D), BF16),
        v((4, Q, 128), F32),
        v((4, Q, 128), F32),
        v((2, Q, 128), F32),
        v((4, Q, 128), F32),
        v((2, 4 * Q, HW), BF16),
        v((Q, W), F32),
        v((4 * Q, W), BF16),
        v((N, N, 16, HW), BF16),
        v((N, N, 16, HW), BF16),
        v((2, HOPS - 1, N, 16, HW), BF16),
        v((2, HOPS - 1, N, 16, HW), BF16),
        v((2, N, 16, QW), BF16),
        v((2, N, 16, QW), BF16),
        v((N, 16, HW), BF16),
        v((N, 16, HW), BF16),
        v((N, 16, HW), BF16),
        v((N, 16, HW), BF16),
        v((Q, D), F32),
        v((Q, D), BF16),
        v((4 * Q, 2 * HB), BF16),
        v((HB, D), BF16),
        v((HB, D), BF16),
        v((HB, D), F32),
        v((HB, D), BF16),
        v((4, D), BF16),
        dma((5,)),
        dma((6,)), dma((6,)),
        dma((1,)), dma((1,)),
        dma((3,)), dma((3,)),
        dma((N,)), dma((N,)), dma((N,)), dma((N,)),
        dma((4, HOPS)), dma((4, HOPS)),
        dma((5,)), dma((5,)),
        dma((3,)), dma((3,)),
        dma((6,)), dma((6,)),
        dma((1,)), dma((1,)),
        dma((4, HOPS)), dma((4, HOPS)),
        dma((N,)), dma((N,)), dma((N,)), dma((N,)),
    ]
    hbm = pl.BlockSpec(memory_space=pl.ANY)
    vmem = pl.BlockSpec(memory_space=pltpu.VMEM)
    return pl.pallas_call(
        kernel,
        out_shape=(
            jax.ShapeDtypeStruct((Q, D), BF16),
            jax.ShapeDtypeStruct((4, D), BF16),
            jax.ShapeDtypeStruct((HB, D), BF16),
        ),
        in_specs=[hbm, vmem, hbm, vmem, vmem, vmem],
        out_specs=(hbm, hbm, hbm),
        scratch_shapes=scratch,
        compiler_params=pltpu.CompilerParams(
            collective_id=0, has_side_effects=True, vmem_limit_bytes=48 * 1024 * 1024
        ),
        cost_estimate=pl.CostEstimate(flops=2_500_000_000, bytes_accessed=3_000_000, transcendentals=200_000),
    )(queries, passages, pool, positives.reshape(1, Q), weights.reshape(1, Q), requests)


def solution(mesh):
    rows = P(("group", "member"), None)
    flat = P(("group", "member"))
    return jax.shard_map(
        per_device,
        mesh=mesh,
        in_specs=(rows, rows, rows, flat, flat, rows),
        out_specs=(rows, rows, rows),
        check_vma=False,
    )
```

time: 526 us -> 77.2 us (0.15)
  blocking collectives: 357 us -> 0 us
  waiting for transfers between devices: 122 us -> 0 us
  Pallas kernels: 0 us -> 70.2 us
  matrix products: 22.7 us -> 0 us
  between operations: 15.2 us -> 0.67 us
    unnamed x2 -> x0, blocking collectives: 343 us -> none
    all_gather x3 -> x0, waiting for transfers between devices: 120 us -> none  [the longest x1 70.5 us: per_device(): batch = lax.all_gather(passages, 'member', axis=0, tiled=True)]
    pallas_call x0 -> x1, Pallas kernels: none -> 70.2 us  [per_device(): pl.pallas_call(kernel, out_shape=(jax.ShapeDtypeStruct((Q, D), BF16), jax...]
    dot_general x6 -> x0, matrix products: 22.7 us -> none  [the longest x1 6.57 us: per_device(): jnp.einsum('qh,qd->hd', far_coefs, visitors, preferred_element_type=jnp.f...]
    all_gather x1 -> x0, blocking collectives: 13.8 us -> none  [per_device(): lax.all_gather(requests, 'group', axis=0, tiled=True)]
  transfers between devices with their start and end apart: 3 -> 0, of which waited for: 2 -> 0; matrix products, arithmetic and copies ran while one was open for 5% -> 0% of each run, Pallas kernels for 0% -> 0%
where the time goes in v1:
time: 77.2 us; the launch traced here: 76.9 us
  Pallas kernels  70.2 us (91%)
  local copies, waits for them, and re-layouts  5.97 us (8%)
    pallas_call x1, Pallas kernels, per_device(): pl.pallas_call(kernel, out_shape=(jax.ShapeDtypeStruct((Q, D), BF16), jax...  70.2 us
    unnamed x15, local copies, waits for them, and re-layouts  5.97 us

profile of v1, /device:TPU:2, one launch (start us, length us, event | category | flops | bytes accessed | tf_op | source)
XLA Modules:
  0.0 76.9 jit_solution(726254109935398666)
XLA Ops:
  0.6 0.0 copy-start.3
  0.6 0.0 copy-start.4
  0.7 0.0 copy-start.5
  0.7 0.6 copy-done.3
  1.3 0.0 copy-done.4
  1.3 0.0 copy-done.5
  1.3 0.0 copy-start
  1.3 1.2 %copy-done = bf16[128,4096]{1,0:T(8,128)(2,1)S(1)} copy-done((bf16[128,4096]{1,0:T(8,128)(2,1)S(1)}, bf16[128,4096]{1,0:T(8,128)(2,1)}, u32[]{:S(2)}) %copy-start) | copy-done | bytes 1048600
  2.5 0.0 copy-start.1
  2.5 1.0 %copy-done.1 = bf16[48,4096]{1,0:T(8,128)(2,1)S(1)} copy-done((bf16[48,4096]{1,0:T(8,128)(2,1)S(1)}, bf16[48,4096]{1,0:T(8,128)(2,1)}, u32[]{:S(2)}) %copy-start.1) | copy-done | bytes 393240
  3.5 0.0 copy-start.2
  3.5 0.8 copy-done.2
  4.3 70.2 %shard_map.85 = (bf16[48,4096]{1,0:T(8,128)(2,1)S(1)}, bf16[4,4096]{1,0:T(4,128)(2,1)S(1)}, bf16[128,4096]{1,0:T(8,128)(2,1)S(1)}) custom-call(bf16[48,4096]{1,0:T(8,128)(2,1)S(1)} %copy-done.1, bf16[4,4096]{1,0:T(4,128)(2,1)S(1)} %copy-done.2, bf16[128,4096]{1,0:T(8,128)(2,1)S(1)} %copy-done, s32[1,48]{1,0:T(1,128)S(1)} %bitcast.2, f32[1,48]{1,0:T(1,128)S(1)} %bitcast.3, ...), custom_call_target="tpu_custom_call" | custom-call | flops 2500000000 | bytes 3000000 | tf_op jit(solution)/shard_map/pallas_call | solution.py:505
  74.5 0.7 copy.12
  75.3 0.6 copy.13
  75.9 1.0 %copy.14 = bf16[128,4096]{1,0:T(8,128)(2,1)} copy(bf16[128,4096]{1,0:T(8,128)(2,1)S(1)} %get-tuple-element.8) | data formatting | bytes 2097152
Async XLA Ops:
  0.6 0.7 copy-start.3
  0.6 0.7 copy-start.4
  0.7 0.7 copy-start.5
  1.3 1.2 %copy-start = (bf16[128,4096]{1,0:T(8,128)(2,1)S(1)}, bf16[128,4096]{1,0:T(8,128)(2,1)}, u32[]{:S(2)}) copy-start(bf16[128,4096]{1,0:T(8,128)(2,1)} %pool_ref.1) | copy-start | bytes 3145732
  2.5 1.0 %copy-start.1 = (bf16[48,4096]{1,0:T(8,128)(2,1)S(1)}, bf16[48,4096]{1,0:T(8,128)(2,1)}, u32[]{:S(2)}) copy-start(bf16[48,4096]{1,0:T(8,128)(2,1)} %q_ref.1) | copy-start | bytes 1179652
  3.5 0.8 copy-start.2

commit v2 on v1

v2 whole, which is shorter than its diff:
```python
import jax
import jax.numpy as jnp
from jax import lax
from jax.experimental import pallas as pl
from jax.experimental.pallas import tpu as pltpu
from jax.sharding import PartitionSpec as P

MESH = pl.DeviceIdType.MESH
F32 = jnp.float32
BF16 = jnp.bfloat16

D = 4096
Q = 48
HB = 128
W = 1024
HW = 512
HALF = D // 2
N = 8
HOPS = N // 2
FACTOR = D ** (-0.5)
NEG = -1e30
VMEM_LIMIT = 40 * 1024 * 1024


def nt(a, b):
    return lax.dot_general(a, b, (((1,), (1,)), ((), ())), preferred_element_type=F32)


def nn(a, b):
    return lax.dot_general(a, b, (((1,), (0,)), ((), ())), preferred_element_type=F32)


def tn(a, b):
    return lax.dot_general(a, b, (((0,), (0,)), ((), ())), preferred_element_type=F32)


def slot_of(rel):
    rel = rel % N
    return 0 if rel == 0 else (2 * rel - 1 if rel <= HOPS else 2 * (N - rel))


def rel_of(slot):
    return (slot + 1) // 2 if slot % 2 else (N - slot // 2) % N


SUM_PIECES = (6, 4, 2, 0)


def loop(n, body):
    lax.fori_loop(0, n, lambda i, _: (body(i), 0)[1], 0)


def cols(i, size):
    return pl.ds(pl.multiple_of(i * size, size), size)


def kernel(
    q_ref, p_ref, pool_ref, pos_ref, w_ref, req_ref,
    gq_ref, gp_ref, gpool_ref,
    q_all, pool2, ga, gb, meta, sc, pb, part, rx, st_out, st, ls, p_in, pos_in, w_in, req_in,
    q4, tin, cin, gpa, gpb, ra, rb, sa, sb, sa_in, sb_in,
    gq_acc, cb, gpo_out, gpo_in, gpo_acc,
    loc, qs, qr, ps, pr, ms, mr, a1s, a1r, b1s, b1r, ags, agr, sts, str_, lss, lsr,
    pts, ptr, gps, gpr, rss, rsr, a2s, a2r, b2s, b2r,
):
    g = lax.axis_index("group")
    mem = lax.axis_index("member")
    x, c = lax.div(g, 2), lax.rem(g, 2)
    y, z = lax.div(mem, N), lax.rem(mem, N)
    right = (lax.rem(x + 1, 4) * 2 + c, mem)
    left = (lax.rem(x + 3, 4) * 2 + c, mem)
    opp = (lax.rem(x + 2, 4) * 2 + c, mem)
    mate_group = x * 2 + 1 - c
    mate = (mate_group, mem)

    def yd(d):
        return (g, lax.rem(y + d, N) * N + z)

    def zd(d):
        return (g, y * N + lax.rem(z + d, N))

    def rc(src, dst, ssem, rsem, dev):
        return pltpu.make_async_remote_copy(
            src_ref=src, dst_ref=dst, send_sem=ssem, recv_sem=rsem,
            device_id=dev, device_id_type=MESH,
        )

    sent = []

    def go(copy):
        copy.start()
        sent.append(copy)

    waited = set()

    def arrived(ref, sem, key=None):
        if key is not None:
            if key in waited:
                return
            waited.add(key)
        rc(ref, ref, sem, sem, right).wait_recv()

    load_p = pltpu.make_async_copy(p_ref, p_in, loc.at[5])
    load_p.start()
    load_req = pltpu.make_async_copy(req_ref, req_in, loc.at[2])
    load_pos = pltpu.make_async_copy(pos_ref, pos_in, loc.at[3])
    load_w = pltpu.make_async_copy(w_ref, w_in, loc.at[4])
    load_req.start()
    load_pos.start()
    load_w.start()
    barrier = pltpu.get_barrier_semaphore()
    for dev in (right, left, opp, mate):
        pl.semaphore_signal(barrier, inc=1, device_id=dev, device_id_type=MESH)
    for d in range(1, N):
        pl.semaphore_signal(barrier, inc=1, device_id=yd(d), device_id_type=MESH)
        pl.semaphore_signal(barrier, inc=1, device_id=zd(d), device_id_type=MESH)

    load_q = pltpu.make_async_copy(q_ref, q_all.at[0], loc.at[0])
    load_pool = pltpu.make_async_copy(pool_ref, pool2.at[pl.ds(0, HB)], loc.at[1])
    load_q.start()
    load_pool.start()

    load_p.wait()
    pf = p_in[...].astype(F32)
    row16 = lax.broadcasted_iota(jnp.int32, (16, HW), 0)

    def fold(off):
        acc = jnp.zeros((16, HW), F32)
        for r in range(4):
            for k in range(4):
                piece = pf[r:r + 1, k * W + off:k * W + off + HW]
                acc = jnp.where(row16 == 4 * r + k, piece, acc)
        return acc.astype(BF16)

    ga[0, 0] = fold(0)
    gb[0, 0] = fold(HW)
    meta[0] = jnp.zeros((8, 128), F32)
    load_req.wait()
    load_pos.wait()
    load_w.wait()
    meta[0, 0:1, 0:8] = req_in[...].astype(F32)

    pl.semaphore_wait(barrier, 4 + 2 * (N - 1))

    for d in (4, 3, 5, 2, 6, 1, 7):
        go(rc(ga.at[0, 0], ga.at[0, slot_of(d)], a1s.at[d], a1r.at[d], zd(d)))
        go(rc(gb.at[0, 0], gb.at[slot_of(d), 0], b1s.at[d], b1r.at[d], yd(d)))
    go(rc(q_ref, q_all.at[1], qs.at[0], qr.at[0], right))
    go(rc(q_ref, q_all.at[2], qs.at[1], qr.at[1], left))
    go(rc(meta.at[0], meta.at[1], ms.at[0], mr.at[0], right))
    go(rc(meta.at[0], meta.at[2], ms.at[1], mr.at[1], left))
    go(rc(meta.at[0], meta.at[3], ms.at[2], mr.at[2], opp))
    go(rc(pool_ref, pool2.at[pl.ds(HB, HB)], ps.at[0], pr.at[0], mate))
    go(rc(q_ref, q_all.at[3], qs.at[2], qr.at[2], opp))

    def ring_view(flow, rel, part):
        near = pl.ds(4 * part, 4)
        return ga.at[slot_of(rel), near] if flow < 2 else gb.at[near, slot_of(rel)]

    def ring_go(flow, src_rel, dst_rel, hops, step, part):
        hop = N - hops if flow % 2 else hops
        sem = 2 * step + part
        go(rc(
            ring_view(flow, src_rel, part), ring_view(flow, dst_rel, part),
            ags.at[flow, sem], agr.at[flow, sem], yd(hop) if flow < 2 else zd(hop),
        ))

    def ring_arrived(flow, step, part):
        rel = (step + 1) * (1 if flow % 2 == 0 else -1)
        arrived(ring_view(flow, rel, part), agr.at[flow, 2 * step + part], ("ring", flow, step, part))

    def ring_step(step, part):
        for flow in range(4):
            sign = 1 if flow % 2 == 0 else -1
            if step == 0:
                for slot in range(max(4 * part, 1), 4 * part + 4):
                    rel = rel_of(slot)
                    if flow < 2:
                        arrived(ga.at[0, slot], a1r.at[rel], ("a1", rel))
                    else:
                        arrived(gb.at[slot, 0], b1r.at[rel], ("b1", rel))
            else:
                ring_arrived(flow, step - 1, part)
            ring_go(flow, sign * step, sign * (step + 1), 1, step, part)
            if step == 2 and flow % 2 == part:
                ring_go(flow, sign * 2, 4, 2, 3, part)

    ring_step(0, 0)
    ring_step(0, 1)

    lane256 = lax.broadcasted_iota(jnp.int32, (1, 2 * HB), 1)
    lane128 = lax.broadcasted_iota(jnp.int32, (1, 128), 1)

    def hard(slot):
        def body(i, acc):
            at = cols(i, 1024)
            return acc + nt(q_all[slot, :, at], pool2[:, at])

        scores = lax.fori_loop(0, 4, body, jnp.zeros((Q, 2 * HB), F32)) * FACTOR
        line = meta[slot, 0:1, :]
        here = jnp.sum(jnp.where(lane128 == g, line, 0.0), axis=1, keepdims=True)
        there = jnp.sum(jnp.where(lane128 == mate_group, line, 0.0), axis=1, keepdims=True)
        asked = jnp.where(lane256 < HB, here, there) != 0.0
        scores = jnp.where(asked, scores, NEG)
        sc[slot] = scores
        top = jnp.max(scores, axis=1, keepdims=True)
        probs = jnp.where(asked, jnp.exp(scores - top), 0.0)
        total = jnp.sum(probs, axis=1, keepdims=True)
        pb[slot] = probs.astype(BF16)
        st_out[slot] = jnp.where(lane128 < 64, top, total)

    def partial(slot, dest, theirs):
        for half in (0, 1):
            def body(i):
                at = cols(i + 4 * half, 512)
                part[slot, :, at] = nn(pb[slot], pool2[:, at]).astype(BF16)

            loop(4, body)
            at, sem = pl.ds(half * HALF, HALF), 2 * theirs + half
            go(rc(part.at[slot, :, at], rx.at[theirs, :, at], pts.at[sem], ptr.at[sem], dest))

    load_q.wait()
    load_pool.wait()
    arrived(pool2.at[pl.ds(HB, HB)], pr.at[0])
    hard(0)
    for k in range(4):
        q4[k * Q:(k + 1) * Q, :] = q_all[0, :, k * W:(k + 1) * W]
    ring_step(1, 0)
    ring_step(1, 1)

    arrived(q_all.at[1], qr.at[0])
    arrived(meta.at[1], mr.at[0])
    hard(1)
    go(rc(st_out.at[1], st.at[2], sts.at[0], str_.at[0], left))
    ring_step(2, 0)
    arrived(q_all.at[2], qr.at[1])
    arrived(meta.at[2], mr.at[1])
    hard(2)
    go(rc(st_out.at[2], st.at[1], sts.at[1], str_.at[1], right))
    ring_step(2, 1)

    arrived(q_all.at[3], qr.at[2])
    arrived(meta.at[3], mr.at[2])
    hard(3)
    go(rc(st_out.at[3], st.at[3], sts.at[2], str_.at[2], opp))
    partial(1, left, 1)
    partial(2, right, 0)

    for flow in range(4):
        for half in (0, 1):
            ring_arrived(flow, 2, half)
        ring_arrived(flow, 3, flow % 2)
    mod4 = lax.rem(lane256, 4)

    def in_block(b):
        pa = ga[pl.ds(2 * b, 2)].reshape(256, HW)
        pbk = gb[pl.ds(2 * b, 2)].reshape(256, HW)
        s = nt(q4[:, 0:HW], pa) + nt(q4[:, HW:W], pbk)
        t = jnp.where(mod4 == 0, s[0:Q], 0.0)
        for k in range(1, 4):
            t = jnp.where(mod4 == k, s[k * Q:(k + 1) * Q], t)
        t = t + jnp.where(lax.rem(mod4, 2) == 0, pltpu.roll(t, 255, 1), pltpu.roll(t, 1, 1))
        t = t + jnp.where(mod4 < 2, pltpu.roll(t, 254, 1), pltpu.roll(t, 2, 1))
        tin[:, cols(b, 256)] = t * FACTOR

    loop(4, in_block)

    for i in range(3):
        arrived(st.at[(2, 1, 3)[i]], str_.at[i])
    tops = [st_out[0][:, 0:1]] + [st[i][:, 0:1] for i in (1, 2, 3)]
    sums = [st_out[0][:, 64:65]] + [st[i][:, 64:65] for i in (1, 2, 3)]
    t_in = tin[...]
    highest = jnp.max(t_in, axis=1, keepdims=True)
    for t in tops:
        highest = jnp.maximum(highest, t)
    lane1024 = lax.broadcasted_iota(jnp.int32, (1, W), 1)
    quarter = lax.rem(lane1024, 4)
    totals = jnp.sum(
        jnp.where(quarter == 0, jnp.exp(t_in - highest), 0.0), axis=1, keepdims=True
    )
    for t, s in zip(tops, sums):
        totals = totals + s * jnp.exp(t - highest)
    logsum = highest + jnp.log(totals)
    eye = lax.broadcasted_iota(jnp.int32, (Q, Q), 0) == lax.broadcasted_iota(jnp.int32, (Q, Q), 1)
    weight = jnp.sum(jnp.where(eye, w_in[...], 0.0), axis=1, keepdims=True)
    positive = jnp.sum(jnp.where(eye, pos_in[...], 0), axis=1, keepdims=True)
    ls[0] = jnp.where(lane128 < 64, logsum, weight)
    go(rc(ls.at[0], ls.at[1], lss.at[0], lsr.at[0], right))
    go(rc(ls.at[0], ls.at[2], lss.at[1], lsr.at[1], left))
    go(rc(ls.at[0], ls.at[3], lss.at[2], lsr.at[2], opp))

    def rel_at(slot):
        half = lax.div(slot + 1, 2)
        return jnp.where(lax.rem(slot, 2) == 1, half, lax.rem(N - half, N))

    from_y = lax.rem(y + N - rel_at(lax.div(lane1024, 128)), N)
    from_z = lax.rem(z + N - rel_at(lax.rem(lax.div(lane1024, 16), N)), N)
    passage = (from_y * N + from_z) * 4 + lax.rem(lax.div(lane1024, 4), 4)
    one_hot = (passage == positive).astype(F32)
    coefs = weight * (jnp.exp(t_in - logsum) - one_hot) * FACTOR
    for k in range(4):
        cin[k * Q:(k + 1) * Q, :] = jnp.where(quarter == k, coefs, 0.0).astype(BF16)

    def gp_block(b):
        rows = tn(cin[:, cols(b, 128)], q4[...]).astype(BF16)
        gpa[b] = rows[:, 0:HW].reshape(N, 16, HW)
        gpb[b] = rows[:, HW:W].reshape(N, 16, HW)

    def sum_view(flow, d, u):
        slot = slot_of(N - d if flow % 2 == 0 else d)
        pair = pl.ds(SUM_PIECES[u], 2)
        return gpa.at[pair, slot] if flow < 2 else gpb.at[slot, pair]

    def sum_slot(flow, kind, u):
        return (ra if flow < 2 else rb).at[flow % 2, kind, pl.ds(SUM_PIECES[u], 2)]

    def sum_go(flow, d, kind, hops, u):
        hop = hops if flow % 2 == 0 else N - hops
        sem = kind * 4 + u
        go(rc(
            sum_view(flow, d, u), sum_slot(flow, kind, u), rss.at[flow, sem], rsr.at[flow, sem],
            zd(hop) if flow < 2 else yd(hop),
        ))

    def sum_add(flow, d, kind, u):
        arrived(sum_slot(flow, kind, u), rsr.at[flow, kind * 4 + u])
        view = sum_view(flow, d, u)
        view[...] = view[...] + sum_slot(flow, kind, u)[...]

    def from_four(flow, u):
        return (u < 2) == (flow % 2 == 0)

    def sum_first(flows):
        for u in range(4):
            for flow in flows:
                if from_four(flow, u):
                    sum_go(flow, 4, 1, 2, u)
                sum_go(flow, 3, 0, 1, u)

    def sum_second():
        for u in range(4):
            for flow in range(4):
                sum_add(flow, 2, 0, u)
                if from_four(flow, u):
                    sum_add(flow, 2, 1, u)
                sum_go(flow, 2, 2, 1, u)

    def sum_third():
        for u in range(4):
            for flow in range(4):
                sum_add(flow, 1, 2, u)
                sum_go(flow, 1, 3, 1, u)

    loop(3, lambda i: gp_block(N - 1 - i))
    sum_first((2, 3))
    loop(N - 3, gp_block)
    sum_first((0, 1))

    partial(3, opp, 2)

    def coef_rows(slot):
        lsum, wt = ls[slot][:, 0:1], ls[slot][:, 64:65]
        cb[slot * Q:(slot + 1) * Q, :] = (wt * jnp.exp(sc[slot] - lsum) * FACTOR).astype(BF16)

    coef_rows(0)

    def own_rows(i):
        at = cols(i, 512)
        gq_acc[:, at] = nn(cb[0:Q, :], pool2[:, at])

    loop(8, own_rows)

    sum_second()

    for h, ref in ((0, ga), (1, gb)):
        for n in range(2):
            rows = nn(cin[...], ref[:, :, :, n * 256:(n + 1) * 256].reshape(W, 256))
            for k in range(4):
                to = pl.ds(k * W + h * HW + n * 256, 256)
                gq_acc[:, to] = gq_acc[:, to] + rows[k * Q:(k + 1) * Q]

    sum_third()

    for i in range(3):
        arrived(ls.at[i + 1], lsr.at[i])
        coef_rows(i + 1)

    def far_pool(i):
        at = cols(i, 512)
        gpo_out[:, at] = tn(cb[:, HB:2 * HB], q_all[:, :, at].reshape(4 * Q, 512)).astype(BF16)

    loop(8, far_pool)
    go(rc(gpo_out, gpo_in, gps.at[0], gpr.at[0], mate))

    def near_pool(i):
        at = cols(i, 512)
        gpo_acc[:, at] = tn(cb[:, 0:HB], q_all[:, :, at].reshape(4 * Q, 512))

    for u in range(4):
        for flow in range(4):
            arrived(sum_slot(flow, 3, u), rsr.at[flow, 12 + u])
        first = SUM_PIECES[u]
        pair = pl.ds(first, 2)
        sa[pair] = (
            gpa[pair, 0].astype(F32) + ra[0, 3, pair].astype(F32)
            + ra[1, 3, pair].astype(F32)
        ).astype(BF16)
        sb[pair] = (
            gpb[0, pair].astype(F32) + rb[0, 3, pair].astype(F32)
            + rb[1, 3, pair].astype(F32)
        ).astype(BF16)
        for slot in (first + 1, first):
            if slot > 0:
                d = N - rel_of(slot)
                go(rc(sa.at[slot], sa_in.at[slot], a2s.at[slot], a2r.at[slot], yd(d)))
                go(rc(sb.at[slot], sb_in.at[slot], b2s.at[slot], b2r.at[slot], zd(d)))

    loop(8, near_pool)
    arrived(gpo_in, gpr.at[0])

    def pool_sum(i):
        at = cols(i, 512)
        gpool_ref[:, at] = (gpo_acc[:, at] + gpo_in[:, at].astype(F32)).astype(BF16)

    loop(8, pool_sum)

    scales = [weight * FACTOR * jnp.exp(t - logsum) for t in tops[1:]]
    for half in (0, 1):
        for way in range(3):
            arrived(rx.at[way, :, pl.ds(half * HALF, HALF)], ptr.at[2 * way + half])

    def finish(i):
        at = cols(i, 512)
        acc = gq_acc[:, at]
        for way in range(3):
            acc = acc + rx[way, :, at].astype(F32) * scales[way]
        gq_ref[:, at] = acc.astype(BF16)

    loop(8, finish)

    row4 = lax.broadcasted_iota(jnp.int32, (4, HW), 0)
    for h, own, held, sem in ((0, sa[0], sa_in, a2r), (1, sb[0], sb_in, b2r)):
        acc = own.astype(F32)
        for slot in range(1, N):
            arrived(held.at[slot], sem.at[slot])
            acc = acc + held[slot].astype(F32)
        for k in range(4):
            out = jnp.zeros((4, HW), F32)
            for r in range(4):
                out = jnp.where(row4 == r, acc[4 * r + k:4 * r + k + 1, :], out)
            gp_ref[:, k * W + h * HW:k * W + (h + 1) * HW] = out.astype(BF16)

    for copy in sent:
        copy.wait_send()


def store(q_in, p_in, pool_in, q_out, p_out, pool_out, sem):
    pairs = ((pool_in, pool_out), (q_in, q_out), (p_in, p_out))
    copies = [pltpu.make_async_copy(src, dst, sem.at[i]) for i, (src, dst) in enumerate(pairs)]
    for copy in copies:
        copy.start()
    for copy in copies:
        copy.wait()


def per_device(queries, passages, pool, positives, weights, requests):
    dma = pltpu.SemaphoreType.DMA
    v = pltpu.VMEM
    scratch = [
        v((4, Q, D), BF16),
        v((2 * HB, D), BF16),
        v((N, N, 16, HW), BF16),
        v((N, N, 16, HW), BF16),
        v((4, 8, 128), F32),
        v((4, Q, 2 * HB), F32),
        v((4, Q, 2 * HB), BF16),
        v((4, Q, D), BF16),
        v((3, Q, D), BF16),
        v((4, Q, 128), F32),
        v((4, Q, 128), F32),
        v((4, Q, 128), F32),
        v((4, D), BF16),
        v((1, Q), jnp.int32),
        v((1, Q), F32),
        v((1, 8), jnp.int32),
        v((4 * Q, W), BF16),
        v((Q, W), F32),
        v((4 * Q, W), BF16),
        v((N, N, 16, HW), BF16),
        v((N, N, 16, HW), BF16),
        v((2, 4, N, 16, HW), BF16),
        v((2, 4, N, 16, HW), BF16),
        v((N, 16, HW), BF16),
        v((N, 16, HW), BF16),
        v((N, 16, HW), BF16),
        v((N, 16, HW), BF16),
        v((Q, D), F32),
        v((4 * Q, 2 * HB), BF16),
        v((HB, D), BF16),
        v((HB, D), BF16),
        v((HB, D), F32),
        dma((6,)),
        dma((3,)), dma((3,)),
        dma((1,)), dma((1,)),
        dma((3,)), dma((3,)),
        dma((N,)), dma((N,)), dma((N,)), dma((N,)),
        dma((4, 8)), dma((4, 8)),
        dma((3,)), dma((3,)),
        dma((3,)), dma((3,)),
        dma((6,)), dma((6,)),
        dma((1,)), dma((1,)),
        dma((4, 16)), dma((4, 16)),
        dma((N,)), dma((N,)), dma((N,)), dma((N,)),
    ]
    hbm = pl.BlockSpec(memory_space=pltpu.HBM)
    vmem = pl.BlockSpec(memory_space=pltpu.VMEM)
    outs = pl.pallas_call(
        kernel,
        out_shape=(
            jax.ShapeDtypeStruct((Q, D), BF16),
            jax.ShapeDtypeStruct((4, D), BF16),
            jax.ShapeDtypeStruct((HB, D), BF16),
        ),
        in_specs=[hbm] * 6,
        out_specs=(vmem,) * 3,
        scratch_shapes=scratch,
        compiler_params=pltpu.CompilerParams(
            collective_id=0, has_side_effects=True, vmem_limit_bytes=VMEM_LIMIT
        ),
        cost_estimate=pl.CostEstimate(flops=2_500_000_000, bytes_accessed=3_000_000, transcendentals=200_000),
    )(*(
        pltpu.with_memory_space_constraint(a, pltpu.HBM)
        for a in (queries, passages, pool, positives.reshape(1, Q), weights.reshape(1, Q), requests)
    ))
    return pl.pallas_call(
        store,
        out_shape=tuple(jax.ShapeDtypeStruct(o.shape, o.dtype) for o in outs),
        in_specs=[vmem] * 3,
        out_specs=(pl.BlockSpec(memory_space=pl.ANY),) * 3,
        scratch_shapes=[dma((3,))],
        compiler_params=pltpu.CompilerParams(vmem_limit_bytes=1024 * 1024),
    )(*outs)


def solution(mesh):
    rows = P(("group", "member"), None)
    flat = P(("group", "member"))
    return jax.shard_map(
        per_device,
        mesh=mesh,
        in_specs=(rows, rows, rows, flat, flat, rows),
        out_specs=(rows, rows, rows),
        check_vma=False,
    )
```

time: 77.2 us -> 67.4 us (0.87)
  the two profiles are of different devices: /device:TPU:2 before, /device:TPU:8 now
where the time goes in v2:
time: 67.4 us; the launch traced here: 67.3 us
  Pallas kernels  66.7 us (99%)
    pallas_call x1, Pallas kernels, per_device(): pl.pallas_call(kernel, out_shape=(jax.ShapeDtypeStruct((Q, D), BF16), jax...  65.5 us

profile of v2, /device:TPU:8, one launch (start us, length us, event | category | flops | bytes accessed | tf_op | source)
XLA Modules:
  0.0 67.3 jit_solution(18280477790087087312)
XLA Ops:
  0.6 65.5 %shard_map.85 = (bf16[48,4096]{1,0:T(8,128)(2,1)S(1)}, bf16[4,4096]{1,0:T(4,128)(2,1)S(1)}, bf16[128,4096]{1,0:T(8,128)(2,1)S(1)}) custom-call(bf16[48,4096]{1,0:T(8,128)(2,1)} %q_ref.1, bf16[4,4096]{1,0:T(4,128)(2,1)} %p_ref.1, bf16[128,4096]{1,0:T(8,128)(2,1)} %pool_ref.1, s32[1,48]{1,0:T(1,128)} %bitcast.2, f32[1,48]{1,0:T(1,128)} %bitcast.3, s32[1,8]{1,0:T(1,128)} %req_ref.1), custom_call_target="tpu_custom_call" | custom-call | flops 2500000000 | bytes 3000000 | tf_op jit(solution)/shard_map/pallas_call | solution.py:517
  66.2 1.1 %shard_map.86 = (bf16[48,4096]{1,0:T(8,128)(2,1)}, bf16[4,4096]{1,0:T(4,128)(2,1)}, bf16[128,4096]{1,0:T(8,128)(2,1)}) custom-call(bf16[48,4096]{1,0:T(8,128)(2,1)S(1)} %get-tuple-element.6.q_in, bf16[4,4096]{1,0:T(4,128)(2,1)S(1)} %get-tuple-element.7.p_in, bf16[128,4096]{1,0:T(8,128)(2,1)S(1)} %get-tuple-element.8.pool_in), custom_call_target="tpu_custom_call" | custom-call | tf_op jit(solution)/shard_map/pallas_call | solution.py:535

commit v3 on v2

--- a/solution.py
+++ b/solution.py
@@ -47,11 +47,12 @@
 
 
 def loop(n, body):
-    lax.fori_loop(0, n, lambda i, _: (body(i), 0)[1], 0)
+    for i in range(n):
+        body(i)
 
 
 def cols(i, size):
-    return pl.ds(pl.multiple_of(i * size, size), size)
+    return pl.ds(i * size, size)
 
 
 def kernel(
@@ -100,6 +101,10 @@
             waited.add(key)
         rc(ref, ref, sem, sem, right).wait_recv()
 
+    def all_sent(copies):
+        for copy in copies:
+            copy.wait_send()
+
     load_p = pltpu.make_async_copy(p_ref, p_in, loc.at[5])
     load_p.start()
     load_req = pltpu.make_async_copy(req_ref, req_in, loc.at[2])
@@ -192,11 +197,7 @@
     lane128 = lax.broadcasted_iota(jnp.int32, (1, 128), 1)
 
     def hard(slot):
-        def body(i, acc):
-            at = cols(i, 1024)
-            return acc + nt(q_all[slot, :, at], pool2[:, at])
-
-        scores = lax.fori_loop(0, 4, body, jnp.zeros((Q, 2 * HB), F32)) * FACTOR
+        scores = nt(q_all[slot], pool2[...]) * FACTOR
         line = meta[slot, 0:1, :]
         here = jnp.sum(jnp.where(lane128 == g, line, 0.0), axis=1, keepdims=True)
         there = jnp.sum(jnp.where(lane128 == mate_group, line, 0.0), axis=1, keepdims=True)
@@ -225,26 +226,25 @@
     hard(0)
     for k in range(4):
         q4[k * Q:(k + 1) * Q, :] = q_all[0, :, k * W:(k + 1) * W]
-    ring_step(1, 0)
-    ring_step(1, 1)
+    for step in (1, 2):
+        ring_step(step, 0)
+        ring_step(step, 1)
 
     arrived(q_all.at[1], qr.at[0])
     arrived(meta.at[1], mr.at[0])
     hard(1)
     go(rc(st_out.at[1], st.at[2], sts.at[0], str_.at[0], left))
-    ring_step(2, 0)
     arrived(q_all.at[2], qr.at[1])
     arrived(meta.at[2], mr.at[1])
     hard(2)
     go(rc(st_out.at[2], st.at[1], sts.at[1], str_.at[1], right))
-    ring_step(2, 1)
 
     arrived(q_all.at[3], qr.at[2])
     arrived(meta.at[3], mr.at[2])
     hard(3)
     go(rc(st_out.at[3], st.at[3], sts.at[2], str_.at[2], opp))
-    partial(1, left, 1)
-    partial(2, right, 0)
+    early = list(sent)
+    sent.clear()
 
     for flow in range(4):
         for half in (0, 1):
@@ -356,6 +356,8 @@
     loop(N - 3, gp_block)
     sum_first((0, 1))
 
+    partial(1, left, 1)
+    partial(2, right, 0)
     partial(3, opp, 2)
 
     def coef_rows(slot):
@@ -379,7 +381,10 @@
                 to = pl.ds(k * W + h * HW + n * 256, 256)
                 gq_acc[:, to] = gq_acc[:, to] + rows[k * Q:(k + 1) * Q]
 
+    later = list(sent)
+    sent.clear()
     sum_third()
+    all_sent(early)
 
     for i in range(3):
         arrived(ls.at[i + 1], lsr.at[i])
@@ -416,6 +421,7 @@
                 go(rc(sb.at[slot], sb_in.at[slot], b2s.at[slot], b2r.at[slot], zd(d)))
 
     loop(8, near_pool)
+    all_sent(later)
     arrived(gpo_in, gpr.at[0])
 
     def pool_sum(i):
@@ -450,8 +456,7 @@
                 out = jnp.where(row4 == r, acc[4 * r + k:4 * r + k + 1, :], out)
             gp_ref[:, k * W + h * HW:k * W + (h + 1) * HW] = out.astype(BF16)
 
-    for copy in sent:
-        copy.wait_send()
+    all_sent(sent)
 
 
 def store(q_in, p_in, pool_in, q_out, p_out, pool_out, sem):

time: 67.4 us -> 62.7 us (0.930)
  the two profiles are of different devices: /device:TPU:8 before, /device:TPU:4 now
where the time goes in v3:
time: 62.7 us; the launch traced here: 62.5 us
  Pallas kernels  61.9 us (99%)
  between operations  0.64 us (1%)
    pallas_call x1, Pallas kernels, per_device(): pl.pallas_call(kernel, out_shape=(jax.ShapeDtypeStruct((Q, D), BF16), jax...  60.8 us

profile of v3, /device:TPU:4, one launch (start us, length us, event | category | flops | bytes accessed | tf_op | source)
XLA Modules:
  0.0 62.5 jit_solution(5941475365861220013)
XLA Ops:
  0.6 60.8 %shard_map.85 = (bf16[48,4096]{1,0:T(8,128)(2,1)S(1)}, bf16[4,4096]{1,0:T(4,128)(2,1)S(1)}, bf16[128,4096]{1,0:T(8,128)(2,1)S(1)}) custom-call(bf16[48,4096]{1,0:T(8,128)(2,1)} %q_ref.1, bf16[4,4096]{1,0:T(4,128)(2,1)} %p_ref.1, bf16[128,4096]{1,0:T(8,128)(2,1)} %pool_ref.1, s32[1,48]{1,0:T(1,128)} %bitcast.2, f32[1,48]{1,0:T(1,128)} %bitcast.3, s32[1,8]{1,0:T(1,128)} %req_ref.1), custom_call_target="tpu_custom_call" | custom-call | flops 2500000000 | bytes 3000000 | tf_op jit(solution)/shard_map/pallas_call | solution.py:522
  61.4 1.1 %shard_map.86 = (bf16[48,4096]{1,0:T(8,128)(2,1)}, bf16[4,4096]{1,0:T(4,128)(2,1)}, bf16[128,4096]{1,0:T(8,128)(2,1)}) custom-call(bf16[48,4096]{1,0:T(8,128)(2,1)S(1)} %get-tuple-element.6.q_in, bf16[4,4096]{1,0:T(4,128)(2,1)S(1)} %get-tuple-element.7.p_in, bf16[128,4096]{1,0:T(8,128)(2,1)S(1)} %get-tuple-element.8.pool_in), custom_call_target="tpu_custom_call" | custom-call | tf_op jit(solution)/shard_map/pallas_call | solution.py:540

commit v4 on v3

--- a/solution.py
+++ b/solution.py
@@ -150,13 +150,15 @@
     for d in (4, 3, 5, 2, 6, 1, 7):
         go(rc(ga.at[0, 0], ga.at[0, slot_of(d)], a1s.at[d], a1r.at[d], zd(d)))
         go(rc(gb.at[0, 0], gb.at[slot_of(d), 0], b1s.at[d], b1r.at[d], yd(d)))
-    go(rc(q_ref, q_all.at[1], qs.at[0], qr.at[0], right))
-    go(rc(q_ref, q_all.at[2], qs.at[1], qr.at[1], left))
+    h0, h1 = pl.ds(0, HALF), pl.ds(HALF, HALF)
+    go(rc(q_ref.at[:, h0], q_all.at[1, :, h0], qs.at[0], qr.at[0], right))
+    go(rc(q_ref.at[:, h1], q_all.at[2, :, h1], qs.at[1], qr.at[1], left))
     go(rc(meta.at[0], meta.at[1], ms.at[0], mr.at[0], right))
     go(rc(meta.at[0], meta.at[2], ms.at[1], mr.at[1], left))
     go(rc(meta.at[0], meta.at[3], ms.at[2], mr.at[2], opp))
     go(rc(pool_ref, pool2.at[pl.ds(HB, HB)], ps.at[0], pr.at[0], mate))
-    go(rc(q_ref, q_all.at[3], qs.at[2], qr.at[2], opp))
+    go(rc(q_ref.at[:, h1], q_all.at[1, :, h1], qs.at[2], qr.at[2], right))
+    go(rc(q_ref.at[:, h0], q_all.at[2, :, h0], qs.at[3], qr.at[3], left))
 
     def ring_view(flow, rel, part):
         near = pl.ds(4 * part, 4)
@@ -196,6 +198,15 @@
     lane256 = lax.broadcasted_iota(jnp.int32, (1, 2 * HB), 1)
     lane128 = lax.broadcasted_iota(jnp.int32, (1, 128), 1)
 
+    row8 = lax.broadcasted_iota(jnp.int32, (8, 1), 0)
+    diagonal = lax.broadcasted_iota(jnp.int32, (Q, 1), 0) == lane128
+
+    def as_row(column):
+        return jnp.sum(jnp.where(diagonal, column, 0.0), axis=0, keepdims=True)
+
+    def as_column(row):
+        return jnp.sum(jnp.where(diagonal, row, 0.0), axis=1, keepdims=True)
+
     def hard(slot):
         scores = nt(q_all[slot], pool2[...]) * FACTOR
         line = meta[slot, 0:1, :]
@@ -208,7 +219,7 @@
         probs = jnp.where(asked, jnp.exp(scores - top), 0.0)
         total = jnp.sum(probs, axis=1, keepdims=True)
         pb[slot] = probs.astype(BF16)
-        st_out[slot] = jnp.where(lane128 < 64, top, total)
+        st_out[slot] = jnp.where(row8 == 0, as_row(top), as_row(total))
 
     def partial(slot, dest, theirs):
         for half in (0, 1):
@@ -226,20 +237,25 @@
     hard(0)
     for k in range(4):
         q4[k * Q:(k + 1) * Q, :] = q_all[0, :, k * W:(k + 1) * W]
+    arrived(q_all.at[1, :, h0], qr.at[0])
+    go(rc(q_all.at[1, :, h0], q_all.at[3, :, h0], qs.at[4], qr.at[4], right))
+    arrived(q_all.at[2, :, h1], qr.at[1])
+    go(rc(q_all.at[2, :, h1], q_all.at[3, :, h1], qs.at[5], qr.at[5], left))
     for step in (1, 2):
         ring_step(step, 0)
         ring_step(step, 1)
 
-    arrived(q_all.at[1], qr.at[0])
+    arrived(q_all.at[1, :, h1], qr.at[2])
     arrived(meta.at[1], mr.at[0])
     hard(1)
     go(rc(st_out.at[1], st.at[2], sts.at[0], str_.at[0], left))
-    arrived(q_all.at[2], qr.at[1])
+    arrived(q_all.at[2, :, h0], qr.at[3])
     arrived(meta.at[2], mr.at[1])
     hard(2)
     go(rc(st_out.at[2], st.at[1], sts.at[1], str_.at[1], right))
 
-    arrived(q_all.at[3], qr.at[2])
+    arrived(q_all.at[3, :, h0], qr.at[4])
+    arrived(q_all.at[3, :, h1], qr.at[5])
     arrived(meta.at[3], mr.at[2])
     hard(3)
     go(rc(st_out.at[3], st.at[3], sts.at[2], str_.at[2], opp))
@@ -267,8 +283,9 @@
 
     for i in range(3):
         arrived(st.at[(2, 1, 3)[i]], str_.at[i])
-    tops = [st_out[0][:, 0:1]] + [st[i][:, 0:1] for i in (1, 2, 3)]
-    sums = [st_out[0][:, 64:65]] + [st[i][:, 64:65] for i in (1, 2, 3)]
+    found = [st_out[0]] + [st[i] for i in (1, 2, 3)]
+    tops = [as_column(f[0:1]) for f in found]
+    sums = [as_column(f[1:2]) for f in found]
     t_in = tin[...]
     highest = jnp.max(t_in, axis=1, keepdims=True)
     for t in tops:
@@ -481,8 +498,8 @@
         v((4, Q, 2 * HB), BF16),
         v((4, Q, D), BF16),
         v((3, Q, D), BF16),
-        v((4, Q, 128), F32),
-        v((4, Q, 128), F32),
+        v((4, 8, 128), F32),
+        v((4, 8, 128), F32),
         v((4, Q, 128), F32),
         v((4, D), BF16),
         v((1, Q), jnp.int32),
@@ -505,7 +522,7 @@
         v((HB, D), BF16),
         v((HB, D), F32),
         dma((6,)),
-        dma((3,)), dma((3,)),
+        dma((6,)), dma((6,)),
         dma((1,)), dma((1,)),
         dma((3,)), dma((3,)),
         dma((N,)), dma((N,)), dma((N,)), dma((N,)),

time: 62.7 us -> 61.5 us (0.981)
  the two profiles are of different devices: /device:TPU:4 before, /device:TPU:8 now
where the time goes in v4:
time: 61.5 us; the launch traced here: 61.4 us
  Pallas kernels  60.7 us (99%)
  between operations  0.64 us (1%)
    pallas_call x1, Pallas kernels, per_device(): pl.pallas_call(kernel, out_shape=(jax.ShapeDtypeStruct((Q, D), BF16), jax...  59.6 us

profile of v4, /device:TPU:8, one launch (start us, length us, event | category | flops | bytes accessed | tf_op | source)
XLA Modules:
  0.0 61.4 jit_solution(11492846830935653233)
XLA Ops:
  0.6 59.6 %shard_map.85 = (bf16[48,4096]{1,0:T(8,128)(2,1)S(1)}, bf16[4,4096]{1,0:T(4,128)(2,1)S(1)}, bf16[128,4096]{1,0:T(8,128)(2,1)S(1)}) custom-call(bf16[48,4096]{1,0:T(8,128)(2,1)} %q_ref.1, bf16[4,4096]{1,0:T(4,128)(2,1)} %p_ref.1, bf16[128,4096]{1,0:T(8,128)(2,1)} %pool_ref.1, s32[1,48]{1,0:T(1,128)} %bitcast.2, f32[1,48]{1,0:T(1,128)} %bitcast.3, s32[1,8]{1,0:T(1,128)} %req_ref.1), custom_call_target="tpu_custom_call" | custom-call | flops 2500000000 | bytes 3000000 | tf_op jit(solution)/shard_map/pallas_call | solution.py:539
  60.3 1.1 %shard_map.86 = (bf16[48,4096]{1,0:T(8,128)(2,1)}, bf16[4,4096]{1,0:T(4,128)(2,1)}, bf16[128,4096]{1,0:T(8,128)(2,1)}) custom-call(bf16[48,4096]{1,0:T(8,128)(2,1)S(1)} %get-tuple-element.6.q_in, bf16[4,4096]{1,0:T(4,128)(2,1)S(1)} %get-tuple-element.7.p_in, bf16[128,4096]{1,0:T(8,128)(2,1)S(1)} %get-tuple-element.8.pool_in), custom_call_target="tpu_custom_call" | custom-call | tf_op jit(solution)/shard_map/pallas_call | solution.py:557
